TPU v7x, 256 devices: a whole 4x4x8 slice. The times are simulated.
256 devices in a mesh: band: 4 (over x), region: 64 (over z, y, core).
Axes of the slice: x: 4, y: 4, z: 8, core: 2. Of those that a mesh axis runs over, the one named last changes fastest.
Arguments:
- fields: float32 [65536, 512], P(('band', 'region')), may hold values from -6 to 6
- send_list: int32 [4, 64, 4, 2], replicated, may hold values from -1 to 1, as said below
- departure: int32 [16, 65536], P(None, ('band', 'region')), may hold values from 0 to 1279, as said below
- hweight: float32 [16, 65536], P(None, ('band', 'region')), may hold values from -0.2 to 0.5
- base_level: int32 [128, 65536], P(None, ('band', 'region')), may hold values from 1 to 125
- vweight: float32 [4, 128, 65536], P(None, None, ('band', 'region')), may hold values from -0.25 to 0.75
- vertical_op: float32 [128, 128], replicated, may hold values from -0.4 to 2, as said below
Outputs:
- level_shards: float32 [512, 65536], P('region', 'band')
Inputs may be any that keep to these rules, and one draw needn't show every extreme that they name: send_list[b, r, d] names distinct block numbers of device (b, r), each block being 128 consecutive points of it; a list holds 1 to 2 numbers followed by -1 in the remaining entries, and in every draw some region's lists are all full. departure[c, p] indexes the extended rows of point p's device: below 256 the device's own point, else 256 + d * 2 * 128 + s for row s of part d; only rows delivered by an existing neighbour from a list entry that is not -1 are named. vertical_op[k, l] is zero where k and l differ by more than 2.
All inputs are finite; a program needn't handle non-finite values.
Results may differ from a plain program's by a relative error of at most 0.0003.
Values sent between devices are 32-bit elements; how exact they have to be, the bound alone decides.
A program may use at most 64 MiB of HBM per device.

v0:
```python
import jax
import jax.numpy as jnp
from jax import lax
from jax.sharding import PartitionSpec as P

BLK = 128


exact_mode = lax.Precision.HIGHEST


def from_behind(block, axis, distance):
    devices = range(lax.axis_size(axis))
    route = [(i - distance, i) for i in devices if i - distance in devices]
    return lax.ppermute(block, axis, route)


def from_behind_2(block, axis, distance):
    devices = range(lax.axis_size(axis))
    route = [((i - distance) % len(devices), i) for i in devices]
    return lax.ppermute(block, axis, route)


def pack_blocks(block_table, block_list):
    safe_list = jnp.maximum(block_list, 0)
    picked = jnp.take(block_table, safe_list, axis=0)
    keeping = (block_list >= 0)[:, None, None]
    picked = jnp.where(keeping, picked, jnp.zeros((), picked.dtype))
    return picked.reshape(-1, picked.shape[-1])


def column_update(extended, depart_block, hweight_block, base_block, vweight_block, vertical_op):
    stencil_len, point_count = depart_block.shape
    width_all = extended.shape[1]
    levels = vertical_op.shape[0]
    fields_count = width_all // levels
    picked = jnp.take(extended, depart_block.reshape(-1), axis=0).reshape(
        stencil_len, point_count, width_all
    )
    horizontal = jnp.sum(hweight_block[:, :, None] * picked, axis=0)
    stacked = jnp.transpose(horizontal).reshape(fields_count, levels, point_count)
    source_ids = jnp.arange(levels, dtype=jnp.int32)[None, :, None]
    level_weights = jnp.zeros((levels, levels, point_count), jnp.float32)
    for offset in range(4):
        target = (base_block + (offset - 1))[:, None, :]
        level_weights = level_weights + jnp.where(
            target == source_ids, vweight_block[offset][:, None, :], jnp.zeros((), jnp.float32)
        )
    interpolated = jnp.einsum("klp,flp->fkp", level_weights, stacked, precision=exact_mode)
    interpolated = jnp.einsum("kl,flp->fkp", vertical_op, interpolated, precision=exact_mode)
    return interpolated.reshape(width_all, point_count)


def body(fields, send_list, departure, hweight, base_level, vweight, vertical_op):
    point_total, width_all = fields.shape
    block_table = fields.reshape(point_total // BLK, BLK, width_all)
    band_id = lax.axis_index("band")
    region_id = lax.axis_index("region")
    own_lists = send_list[band_id, region_id]
    from_north = from_behind(pack_blocks(block_table, own_lists[0]), "band", 1)
    from_south = from_behind(pack_blocks(block_table, own_lists[1]), "band", -1)
    from_west = from_behind_2(pack_blocks(block_table, own_lists[2]), "region", 1)
    from_east = from_behind_2(pack_blocks(block_table, own_lists[3]), "region", -1)
    extended = jnp.concatenate([fields, from_north, from_south, from_west, from_east], axis=0)
    step_points = min(128, point_total)

    def one_step(step_id, result):
        first_col = step_id * step_points
        updated = column_update(
            extended,
            lax.dynamic_slice_in_dim(departure, first_col, step_points, 1),
            lax.dynamic_slice_in_dim(hweight, first_col, step_points, 1),
            lax.dynamic_slice_in_dim(base_level, first_col, step_points, 1),
            lax.dynamic_slice_in_dim(vweight, first_col, step_points, 2),
            vertical_op,
        )
        return lax.dynamic_update_slice_in_dim(result, updated, first_col, 1)

    result = lax.fori_loop(
        0, point_total // step_points, one_step, jnp.zeros((width_all, point_total), jnp.float32)
    )
    return lax.all_to_all(result, "region", split_axis=0, concat_axis=1, tiled=True)


def solution(mesh):
    placed = (
        P(("band", "region"), None),
        P(),
        P(None, ("band", "region")),
        P(None, ("band", "region")),
        P(None, ("band", "region")),
        P(None, None, ("band", "region")),
        P(),
    )
    return jax.shard_map(
        body, mesh=mesh, in_specs=placed, out_specs=P("region", "band"), check_vma=False
    )
```

profile of v0, /device:TPU:1, one launch (start us, length us, event | category | flops | bytes accessed | tf_op | source)
XLA Modules:
  0.0 142.0 jit_solution(3975033696603321901)
XLA Ops:
  0.0 1.0 maximum_reduce_fusion
  2.0 1.6 %gather_fusion.1 = f32[2,128,512]{2,1,0:T(8,128)S(1)} fusion(f32[2,128,512]{2,1,0:T(8,128)} %bitcast.57, s32[1024]{0:T(1024)S(1)} %pad_clamp_fusion.3), kind=kCustom, calls=%fused_computation.clone | custom fusion | bytes 1048584 | tf_op jit(solution)/shard_map/jit(_take)/gather | solution.py:26
  4.6 4.7 %collective-permute-start = (f32[256,512]{1,0:T(8,128)}, f32[256,512]{1,0:T(8,128)}, u32[]{:S(2)}, u32[]{:S(2)}) collective-permute-start(f32[256,512]{1,0:T(8,128)} %bitcast.13), channel_id=1, source_target_pairs={{0,64},{64,128},{128,192},{1,65},{65,129},{129,193},{2,66},{66,130... | collective-permute-start | bytes 1572872 | tf_op jit(solution)/shard_map/ppermute | solution.py:15
  9.3 1.6 %gather_fusion.2 = f32[2,128,512]{2,1,0:T(8,128)S(1)} fusion(f32[2,128,512]{2,1,0:T(8,128)} %bitcast.58, s32[1024]{0:T(1024)S(1)} %pad_clamp_fusion.2), kind=kCustom, calls=%fused_computation.2.clone | custom fusion | bytes 1048584 | tf_op jit(solution)/shard_map/jit(_take)/gather | solution.py:26
  11.9 1.3 collective-permute-start.1
  14.8 2.1 %collective-permute-start.2 = (f32[256,512]{1,0:T(8,128)}, f32[256,512]{1,0:T(8,128)}, u32[]{:S(2)}, u32[]{:S(2)}) collective-permute-start(f32[256,512]{1,0:T(8,128)} %bitcast.15), channel_id=1, source_target_pairs={{63,0},{0,1},{1,2},{2,3},{3,4},{4,5},{5,6},{6,7},{7,8},{8,9},{9,10... | collective-permute-start | bytes 1572872 | tf_op jit(solution)/shard_map/ppermute | solution.py:21
  19.4 1.1 constant_dynamic-update-slice_fusion.4
  20.5 6.1 %collective-permute-done.1 = f32[256,512]{1,0:T(8,128)} collective-permute-done((f32[256,512]{1,0:T(8,128)}, f32[256,512]{1,0:T(8,128)}, u32[]{:S(2)}, u32[]{:S(2)}) %collective-permute-start.1) | collective-permute-done | bytes 524320 | tf_op jit(solution)/shard_map/ppermute | solution.py:15
  26.5 1.1 constant_dynamic-update-slice_fusion.3
  27.6 1.1 constant_dynamic-update-slice_fusion.2
  28.7 1.1 constant_dynamic-update-slice_fusion.1
  30.6 79.3 %while.13 = (s32[]{:T(128)}, f32[512,256]{1,0:T(8,128)}, f32[16,256]{1,0:T(8,128)S(1)}, s32[16,256]{1,0:T(8,128)S(1)}, f32[1280,512]{1,0:T(8,128)S(1)}, /*index=...) while((s32[]{:T(128)}, f32[512,256]{1,0:T(8,128)}, ...), condition=%wide.region_2.4_spmd, body=%wide.region_0.3_spmd.sunk | while | flops 227545088 | bytes 50614524 | solution.py:79
  30.7 1.0 dynamic-slice_bitcast_fusion.5
  32.5 6.1 %select_add_fusion.2 = f32[128,128,128]{2,1,0:T(8,128)} fusion(f32[128,128]{1,0:T(8,128)S(1)} %get-tuple-element.249, s32[128,128]{1,0:T(8,128)S(1)} %get-tuple-element.251, f32[128,128]{1,0:T(8,128)S(1)} %get-tuple-element.252, s32[128,128]{1,0:T(8,128)S(1)} %get-tuple-element.253, f32[128,128]{1,0:T(8,128)S(1)} %get-tuple-element.254, ...), kind=kLoop, calls=%fused_computation.5.clone.1 | loop fusion | flops 23068672 | bytes 8912896 | tf_op jit(solution)/shard_map/while/body/eval_jaxpr/add | solution.py:46
  38.6 9.4 %copy.12 = f32[128,128,128]{0,1,2:T(8,128)} copy(f32[128,128,128]{2,1,0:T(8,128)} %select_add_fusion.2) | data formatting | bytes 16777216 | tf_op jit(solution)/shard_map/while/body/eval_jaxpr/add | solution.py:46
  48.0 9.0 %gather_fusion = f32[2048,512]{1,0:T(8,128)} fusion(f32[1280,512]{1,0:T(8,128)S(1)} %get-tuple-element.291, s32[2048]{0:T(1024)S(1)} %broadcast_clamp_fusion.2), kind=kCustom, calls=%fused_computation.1.clone.1 | custom fusion | bytes 8396800 | tf_op jit(solution)/shard_map/while/body/eval_jaxpr/jit(_take)/gather | solution.py:37
  56.9 2.6 %multiply_reduce_fusion.2 = f32[128,512]{1,0:T(8,128)S(1)} fusion(f32[16,128,512]{2,1,0:T(8,128)} %bitcast.54, f32[16,128]{1,0:T(8,128)S(1)} %constant_dynamic-slice_fusion.10, pred[16,128]{1,0:T(8,128)(4,1)S(1)} %get-tuple-element.248), kind=kLoop, calls=%fused_computation.10.clone.1 | loop fusion | flops 3080192 | bytes 4466688 | tf_op jit(solution)/shard_map/while/body/eval_jaxpr/reduce_sum | solution.py:40
  59.7 9.4 %fusion.16 = f32[128,4,128]{2,1,0:T(4,128)S(1)} fusion(f32[4,128,128]{1,0,2:T(4,128)S(1)} %reshape.216, f32[128,128,128]{0,1,2:T(8,128)} %copy.12), kind=kOutput, calls=%fused_computation.62.clone.1 | convolution fusion | flops 100663296 | bytes 8912896 | tf_op jit(solution)/shard_map/while/body/eval_jaxpr/klp,flp->fkp/dot_general | solution.py:49
  72.1 6.1 %select_add_fusion.2 = f32[128,128,128]{2,1,0:T(8,128)} fusion(f32[128,128]{1,0:T(8,128)S(1)} %get-tuple-element.249, s32[128,128]{1,0:T(8,128)S(1)} %get-tuple-element.251, f32[128,128]{1,0:T(8,128)S(1)} %get-tuple-element.252, s32[128,128]{1,0:T(8,128)S(1)} %get-tuple-element.253, f32[128,128]{1,0:T(8,128)S(1)} %get-tuple-element.254, ...), kind=kLoop, calls=%fused_computation.5.clone.1 | loop fusion | flops 23068672 | bytes 8912896 | tf_op jit(solution)/shard_map/while/body/eval_jaxpr/add | solution.py:46
  78.2 9.4 %copy.12 = f32[128,128,128]{0,1,2:T(8,128)} copy(f32[128,128,128]{2,1,0:T(8,128)} %select_add_fusion.2) | data formatting | bytes 16777216 | tf_op jit(solution)/shard_map/while/body/eval_jaxpr/add | solution.py:46
  87.6 9.0 %gather_fusion = f32[2048,512]{1,0:T(8,128)} fusion(f32[1280,512]{1,0:T(8,128)S(1)} %get-tuple-element.291, s32[2048]{0:T(1024)S(1)} %broadcast_clamp_fusion.2), kind=kCustom, calls=%fused_computation.1.clone.1 | custom fusion | bytes 8396800 | tf_op jit(solution)/shard_map/while/body/eval_jaxpr/jit(_take)/gather | solution.py:37
  96.6 2.6 %multiply_reduce_fusion.2 = f32[128,512]{1,0:T(8,128)S(1)} fusion(f32[16,128,512]{2,1,0:T(8,128)} %bitcast.54, f32[16,128]{1,0:T(8,128)S(1)} %constant_dynamic-slice_fusion.10, pred[16,128]{1,0:T(8,128)(4,1)S(1)} %get-tuple-element.248), kind=kLoop, calls=%fused_computation.10.clone.1 | loop fusion | flops 3080192 | bytes 4466688 | tf_op jit(solution)/shard_map/while/body/eval_jaxpr/reduce_sum | solution.py:40
  99.3 9.4 %fusion.16 = f32[128,4,128]{2,1,0:T(4,128)S(1)} fusion(f32[4,128,128]{1,0,2:T(4,128)S(1)} %reshape.216, f32[128,128,128]{0,1,2:T(8,128)} %copy.12), kind=kOutput, calls=%fused_computation.62.clone.1 | convolution fusion | flops 100663296 | bytes 8912896 | tf_op jit(solution)/shard_map/while/body/eval_jaxpr/klp,flp->fkp/dot_general | solution.py:49
  109.9 31.2 %all_to_all.19 = f32[64,8,256]{2,1,0:T(8,128)S(1)} all-to-all(f32[64,8,256]{2,1,0:T(8,128)} %bitcast.61), channel_id=1, replica_groups=mesh['band'=4,'region'=64] {'region'}, dimensions={0} | all-to-all | bytes 1048576 | tf_op jit(solution)/shard_map/all_to_all | solution.py:82
  (51 shorter events, 14.0 us)
Async XLA Ops:
  0.0 13.2 %copy-start = (f32[256,512]{1,0:T(8,128)S(1)}, f32[256,512]{1,0:T(8,128)}, u32[]{:S(2)}) copy-start(f32[256,512]{1,0:T(8,128)} %param.11) | copy-start | bytes 1572868
  4.6 14.8 %collective-permute-start = (f32[256,512]{1,0:T(8,128)}, f32[256,512]{1,0:T(8,128)}, u32[]{:S(2)}, u32[]{:S(2)}) collective-permute-start(f32[256,512]{1,0:T(8,128)} %bitcast.13), channel_id=1, source_target_pairs={{0,64},{64,128},{128,192},{1,65},{65,129},{129,193},{2,66},{66,130... | collective-permute-start | bytes 1572872 | tf_op jit(solution)/shard_map/ppermute | solution.py:15
  11.9 14.7 %collective-permute-start.1 = (f32[256,512]{1,0:T(8,128)}, f32[256,512]{1,0:T(8,128)}, u32[]{:S(2)}, u32[]{:S(2)}) collective-permute-start(f32[256,512]{1,0:T(8,128)} %bitcast.14), channel_id=1, source_target_pairs={{64,0},{128,64},{192,128},{65,1},{129,65},{193,129},{66,2},{130,66... | collective-permute-start | bytes 1572872 | tf_op jit(solution)/shard_map/ppermute | solution.py:15
  14.8 15.9 %copy-start.1 = (f32[128,128]{1,0:T(8,128)S(1)}, f32[128,128]{1,0:T(8,128)}, u32[]{:S(2)}) copy-start(f32[128,128]{1,0:T(8,128)} %param.17) | copy-start | bytes 196612
  14.8 15.9 %copy-start.2 = (s32[16,256]{1,0:T(8,128)S(1)}, s32[16,256]{1,0:T(8,128)}, u32[]{:S(2)}) copy-start(s32[16,256]{1,0:T(8,128)} %param.13) | copy-start | bytes 49156
  14.8 15.9 %copy-start.3 = (f32[16,256]{1,0:T(8,128)S(1)}, f32[16,256]{1,0:T(8,128)}, u32[]{:S(2)}) copy-start(f32[16,256]{1,0:T(8,128)} %param.14) | copy-start | bytes 49156
  14.8 12.9 %collective-permute-start.2 = (f32[256,512]{1,0:T(8,128)}, f32[256,512]{1,0:T(8,128)}, u32[]{:S(2)}, u32[]{:S(2)}) collective-permute-start(f32[256,512]{1,0:T(8,128)} %bitcast.15), channel_id=1, source_target_pairs={{63,0},{0,1},{1,2},{2,3},{3,4},{4,5},{5,6},{6,7},{7,8},{8,9},{9,10... | collective-permute-start | bytes 1572872 | tf_op jit(solution)/shard_map/ppermute | solution.py:21
  18.4 10.3 %collective-permute-start.3 = (f32[256,512]{1,0:T(8,128)}, f32[256,512]{1,0:T(8,128)}, u32[]{:S(2)}, u32[]{:S(2)}) collective-permute-start(f32[256,512]{1,0:T(8,128)} %bitcast.16), channel_id=1, source_target_pairs={{1,0},{2,1},{3,2},{4,3},{5,4},{6,5},{7,6},{8,7},{9,8},{10,9},{11,1... | collective-permute-start | bytes 1572872 | tf_op jit(solution)/shard_map/ppermute | solution.py:21
where the time goes:
time: 143 us; the launch traced here: 142 us
  local copies, waits for them, and re-layouts  50.8 us (36%)
  blocking collectives  31.2 us (22%)
  other arithmetic  24.9 us (17%)
  matrix products  19.6 us (14%)
  starting transfers between devices  8.15 us (6%)
  waiting for transfers between devices  6.99 us (5%)
    all_to_all x1, blocking collectives, body(): lax.all_to_all(result, 'region', split_axis=0, concat_axis=1, tiled=True)  31.2 us
    dot_general x2, matrix products, column_update(): jnp.einsum('klp,flp->fkp', level_weights, stacked, precision=exact_mode)  18.8 us
    add x2, local copies, waits for them, and re-layouts, column_update(): level_weights + jnp.where(target == source_ids, vweight_block[offset][:,...  18.7 us
    gather x2, local copies, waits for them, and re-layouts, column_update(): jnp.take(extended, depart_block.reshape(-1), axis=0)  17.9 us
    add x2, other arithmetic, column_update(): level_weights + jnp.where(target == source_ids, vweight_block[offset][:,...  12.2 us
    ppermute x2, waiting for transfers between devices, from_behind(): return lax.ppermute(block, axis, route)  6.99 us
    ppermute x2, starting transfers between devices, from_behind(): return lax.ppermute(block, axis, route)  6.01 us
    reduce_sum x2, other arithmetic, column_update(): horizontal = jnp.sum(hweight_block[:, :, None] * picked, axis=0)  5.2 us
  transfers between devices with their start and end apart: 4, of which 2 were waited for; matrix products, arithmetic and copies ran while one was open for 6% of the time, Pallas kernels for 0%

commit v1 on v0

v1 whole, which is shorter than its diff:
```python
import functools

import jax
import jax.numpy as jnp
from jax import lax
from jax.experimental import pallas as pl
from jax.experimental.pallas import tpu as pltpu
from jax.sharding import PartitionSpec as P

MESH = pl.DeviceIdType.MESH
LEV = 128
LANES = 128
FAR = 1 << 20
F32, BF16 = jnp.float32, jnp.bfloat16
NT = (((1,), (1,)), ((), ()))


def halves(x):
    high = x.astype(BF16)
    return high, (x - high.astype(F32)).astype(BF16)


def kernel(
    bands, regions, fields, lists, departure, hweight, base_level, vweight, vertical_op, out,
    own, halo, lists_s, dep_v, hw_v, base_v, vw_v, vop_v, dep_t, hw_t, w_f32, w_hi, w_lo, e_cat, base_t, vw_t, made,
    in_sem, halo_send, halo_recv, own_sem, send_sem, recv_sem,
):
    b, r = lax.axis_index("band"), lax.axis_index("region")
    points = fields.shape[0]
    n_fields = fields.shape[1] // LEV
    group = regions // n_fields
    rows = LEV // group
    east, west = lax.rem(r + 1, regions), lax.rem(r + regions - 1, regions)

    loads = [
        pltpu.make_async_copy(src, dst, in_sem.at[i])
        for i, (src, dst) in enumerate(
            [(lists, lists_s), (departure, dep_v), (hweight, hw_v), (base_level, base_v), (vweight, vw_v), (vertical_op, vop_v), (fields, own)]
        )
    ]
    for load in loads:
        load.start()

    barrier = pltpu.get_barrier_semaphore()

    def greet(band, region):
        pl.semaphore_signal(barrier, inc=1, device_id=(band, region), device_id_type=MESH)

    @pl.when(b > 0)
    def _():
        greet(b - 1, r)

    @pl.when(b < bands - 1)
    def _():
        greet(b + 1, r)

    def greet_region(i, carry):
        greet(b, lax.rem(r + i, regions))
        return carry

    lax.fori_loop(1, regions, greet_region, 0)
    pl.semaphore_wait(barrier, regions - 1 + jnp.minimum(b, 1) + jnp.minimum(bands - 1 - b, 1))

    def offset(t):
        return lax.rem(2 + t * (t + 1) // 2, n_fields)

    def field_of(region, t):
        return lax.rem(region // group + offset(t), n_fields)

    def halo_copy(t, d, band, region):
        column = pl.multiple_of(field_of(region, t) * LEV, LEV)
        return pltpu.make_async_remote_copy(
            src_ref=fields.at[:, pl.ds(column, LEV)],
            dst_ref=halo.at[t, d],
            send_sem=halo_send.at[t, d],
            recv_sem=halo_recv.at[t, d],
            device_id=(band, region),
            device_id_type=MESH,
        )

    def send_halo(t, carry):
        @pl.when(b < bands - 1)
        def _():
            halo_copy(t, 0, b + 1, r).start()

        @pl.when(b > 0)
        def _():
            halo_copy(t, 1, b - 1, r).start()

        halo_copy(t, 2, b, east).start()
        halo_copy(t, 3, b, west).start()
        return carry

    lax.fori_loop(0, n_fields, send_halo, 0)

    def blank(d):
        def one(t, carry):
            halo[t, d] = jnp.zeros(halo.shape[2:], F32)
            return carry

        lax.fori_loop(0, n_fields, one, 0)

    @pl.when(b == 0)
    def _():
        blank(0)

    @pl.when(b == bands - 1)
    def _():
        blank(1)

    for load in loads:
        load.wait()

    blocks = points // LANES
    bases = [i * LANES for i in range(blocks)]
    before, after = jnp.maximum(b - 1, 0), jnp.minimum(b + 1, bands - 1)
    for d, (band, region) in enumerate([(before, r), (after, r), (b, west), (b, east)]):
        first, second = (lists_s[band * 4 + d, e, region] for e in range(2))
        part = points + d * points
        for block in range(blocks):
            bases.append(jnp.where(first == block, part, jnp.where(second == block, part + LANES, FAR)))

    dep_t[...] = jnp.transpose(dep_v[...])
    hw_t[...] = jnp.transpose(hw_v[...])
    stencil = dep_v.shape[0]

    def weigh(i, carry):
        rows_i = pl.ds(pl.multiple_of(i * 8, 8), 8)
        dep, hw = dep_t[rows_i, :], hw_t[rows_i, :]
        deps = [jnp.broadcast_to(dep[:, c : c + 1], (8, LANES)) for c in range(stencil)]
        hws = [jnp.broadcast_to(hw[:, c : c + 1], (8, LANES)) for c in range(stencil)]
        lane = lax.broadcasted_iota(jnp.int32, (8, LANES), 1)
        for j, base in enumerate(bases):
            target = lane + base
            total = jnp.where(deps[0] == target, hws[0], 0.0)
            for c in range(1, stencil):
                total = total + jnp.where(deps[c] == target, hws[c], 0.0)
            w_f32[rows_i, j * LANES : (j + 1) * LANES] = total
        return carry

    lax.fori_loop(0, points // 8, weigh, 0)

    def split(i, carry):
        rows_i = pl.ds(pl.multiple_of(i * 16, 16), 16)
        w_hi[rows_i, :], w_lo[rows_i, :] = halves(w_f32[rows_i, :])
        return carry

    lax.fori_loop(0, points // 16, split, 0)

    base_t[...] = jnp.transpose(base_v[...])
    for m in range(4):
        vw_t[m] = jnp.transpose(vw_v[m])
    v_hi, v_lo = halves(vop_v[...])
    v_cat = jnp.concatenate([v_hi, v_hi], axis=1)

    def one_field(t, carry):
        f = field_of(r, t)
        column = pl.multiple_of(f * LEV, LEV)
        e_cat[:points, :LEV], e_cat[:points, LEV:] = halves(own[:, pl.ds(column, LEV)])

        @pl.when(b > 0)
        def _():
            halo_copy(t, 0, b, r).wait_recv()

        @pl.when(b < bands - 1)
        def _():
            halo_copy(t, 1, b, r).wait_recv()

        halo_copy(t, 2, b, r).wait_recv()
        halo_copy(t, 3, b, r).wait_recv()
        for d in range(4):
            part = slice((d + 1) * points, (d + 2) * points)
            e_cat[part, :LEV], e_cat[part, LEV:] = halves(halo[t, d])
        both = jnp.dot(w_hi[...], e_cat[...], preferred_element_type=F32)
        rest = jnp.dot(w_lo[...], e_cat[:, :LEV], preferred_element_type=F32)
        horizontal = both[:, :LEV] + both[:, LEV:] + rest
        mixed = jnp.zeros((points, LEV), F32)
        for m in range(4):
            picked = jnp.take_along_axis(horizontal, base_t[...] + (m - 1), axis=1, mode="promise_in_bounds")
            mixed = mixed + vw_t[m] * picked
        i_hi, i_lo = halves(mixed)
        i_cat = jnp.concatenate([i_hi, i_lo], axis=1)
        made[t] = lax.dot_general(v_cat, i_cat, NT, preferred_element_type=F32) + lax.dot_general(
            v_lo, i_hi, NT, preferred_element_type=F32
        )
        place = pl.ds(pl.multiple_of(r * points, points), points)

        def send_rows(i, carry):
            j = lax.rem(i + r, group)
            target = f * group + j
            src = made.at[t, pl.ds(pl.multiple_of(j * rows, rows), rows)]

            @pl.when(target != r)
            def _():
                pltpu.make_async_remote_copy(
                    src_ref=src,
                    dst_ref=out.at[:, place],
                    send_sem=send_sem,
                    recv_sem=recv_sem,
                    device_id=(b, target),
                    device_id_type=MESH,
                ).start()

            @pl.when(target == r)
            def _():
                pltpu.make_async_copy(src, out.at[:, place], own_sem).start()

            return carry

        lax.fori_loop(0, group, send_rows, 0)
        return carry

    lax.fori_loop(0, n_fields, one_field, 0)

    def halo_sent(t, carry):
        @pl.when(b < bands - 1)
        def _():
            halo_copy(t, 0, b, r).wait_send()

        @pl.when(b > 0)
        def _():
            halo_copy(t, 1, b, r).wait_send()

        halo_copy(t, 2, b, east).wait_send()
        halo_copy(t, 3, b, west).wait_send()
        return carry

    lax.fori_loop(0, n_fields, halo_sent, 0)
    mine = out.at[:, : points]
    pltpu.make_async_copy(mine, mine, own_sem).wait()
    others = out.at[:, : (regions - 1) * points]
    pltpu.make_async_copy(others, others, send_sem).wait()
    pltpu.make_async_copy(others, others, recv_sem).wait()


def solution(mesh):
    bands, regions = mesh.shape["band"], mesh.shape["region"]

    def body(fields, send_list, departure, hweight, base_level, vweight, vertical_op):
        points, width = fields.shape
        n_fields = width // LEV
        stencil = departure.shape[0]
        lists = send_list.transpose(0, 2, 3, 1).reshape(bands * 4, 2, regions)
        extended = points * 5
        anywhere = pl.BlockSpec(memory_space=pl.ANY)
        resident = anywhere
        return pl.pallas_call(
            functools.partial(kernel, bands, regions),
            out_shape=jax.ShapeDtypeStruct((width // regions, points * regions), F32),
            in_specs=[resident] * 7,
            out_specs=anywhere,
            scratch_shapes=[
                pltpu.VMEM((points, width), F32),
                pltpu.VMEM((n_fields, 4, points, LEV), F32),
                pltpu.SMEM(lists.shape, jnp.int32),
                pltpu.VMEM(departure.shape, jnp.int32),
                pltpu.VMEM(hweight.shape, F32),
                pltpu.VMEM(base_level.shape, jnp.int32),
                pltpu.VMEM(vweight.shape, F32),
                pltpu.VMEM(vertical_op.shape, F32),
                pltpu.VMEM((points, stencil), jnp.int32),
                pltpu.VMEM((points, stencil), F32),
                pltpu.VMEM((points, extended), F32),
                pltpu.VMEM((points, extended), BF16),
                pltpu.VMEM((points, extended), BF16),
                pltpu.VMEM((extended, 2 * LEV), BF16),
                pltpu.VMEM((points, LEV), jnp.int32),
                pltpu.VMEM((4, points, LEV), F32),
                pltpu.VMEM((n_fields, LEV, points), F32),
                pltpu.SemaphoreType.DMA((7,)),
                pltpu.SemaphoreType.DMA((n_fields, 4)),
                pltpu.SemaphoreType.DMA((n_fields, 4)),
                pltpu.SemaphoreType.DMA,
                pltpu.SemaphoreType.DMA,
                pltpu.SemaphoreType.DMA,
            ],
            compiler_params=pltpu.CompilerParams(
                collective_id=0, has_side_effects=True, vmem_limit_bytes=63 * 2**20
            ),
            name="semi_lagrangian",
        )(fields, lists, departure, hweight, base_level, vweight, vertical_op)

    points_last = P(None, ("band", "region"))
    return jax.shard_map(
        body,
        mesh=mesh,
        in_specs=(
            P(("band", "region"), None),
            P(),
            points_last,
            points_last,
            points_last,
            P(None, None, ("band", "region")),
            P(),
        ),
        out_specs=P("region", "band"),
        check_vma=False,
    )
```

time: 143 us -> 34.1 us (0.24)
  local copies, waits for them, and re-layouts: 50.8 us -> 1.87 us
  Pallas kernels: 0 us -> 32.1 us
  blocking collectives: 31.2 us -> 0 us
  other arithmetic: 24.9 us -> 0 us
  matrix products: 19.6 us -> 0 us
  starting transfers between devices: 8.15 us -> 0 us
  waiting for transfers between devices: 6.99 us -> 0 us
    pallas_call x0 -> x1, Pallas kernels: none -> 32.1 us  [body(): pl.pallas_call(functools.partial(kernel, bands, regions), out_shape=jax.S...]
    all_to_all x1 -> x0, blocking collectives: 31.2 us -> none  [body(): lax.all_to_all(result, 'region', split_axis=0, concat_axis=1, tiled=True)]
    gather x6 -> x0, local copies, waits for them, and re-layouts: 22.3 us -> none  [the longest x2 17.9 us: column_update(): jnp.take(extended, depart_block.reshape(-1), axis=0)]
    dot_general x4 -> x0, matrix products: 19.6 us -> none  [the longest x2 18.8 us: column_update(): jnp.einsum('klp,flp->fkp', level_weights, stacked, precision=exact_mode)]
    add x2 -> x0, local copies, waits for them, and re-layouts: 18.7 us -> none  [column_update(): level_weights + jnp.where(target == source_ids, vweight_block[offset][:,...]
    add x6 -> x0, other arithmetic: 13.9 us -> none  [the longest x2 12.2 us: column_update(): level_weights + jnp.where(target == source_ids, vweight_block[offset][:,...]
    ppermute x4 -> x0, starting transfers between devices: 8.15 us -> none  [the longest x2 6.01 us: from_behind(): return lax.ppermute(block, axis, route)]
    ppermute x4 -> x0, waiting for transfers between devices: 6.99 us -> none  [the longest x2 6.99 us: from_behind(): return lax.ppermute(block, axis, route)]
  transfers between devices with their start and end apart: 4 -> 0, of which waited for: 2 -> 0; matrix products, arithmetic and copies ran while one was open for 6% -> 0% of each run, Pallas kernels for 0% -> 0%
where the time goes in v1:
time: 34.1 us; the launch traced here: 33.9 us
  Pallas kernels  32.1 us (94%)
  local copies, waits for them, and re-layouts  1.87 us (5%)
    pallas_call x1, Pallas kernels, body(): pl.pallas_call(functools.partial(kernel, bands, regions), out_shape=jax.S...  32.1 us
    unnamed x1, local copies, waits for them, and re-layouts  1.87 us

profile of v1, /device:TPU:1, one launch (start us, length us, event | category | flops | bytes accessed | tf_op | source)
XLA Modules:
  0.0 33.9 jit_solution(2183023668660474641)
XLA Ops:
  0.0 32.1 %semi_lagrangian.1 = f32[8,16384]{1,0:T(8,128)} custom-call(f32[256,512]{1,0:T(8,128)} %fields.1, s32[16,2,64]{2,1,0:T(2,128)} %bitcast.3, s32[16,256]{1,0:T(8,128)} %departure.1, f32[16,256]{1,0:T(8,128)} %hweight.1, s32[128,256]{1,0:T(8,128)} %base_level.1, f32[4,128,256]{2,1,0:T(8,128)} %vweight.1, f32[128,128]{1,0:T(8,128)} %vertical_op.1), custom_call_target="tpu_custom_call" | custom-call | tf_op jit(solution)/shard_map/semi_lagrangian/pallas_call | solution.py:247
  32.1 1.9 %copy.9 = f32[8,16384]{1,0:T(8,128)} copy(f32[8,16384]{1,0:T(8,128)} %semi_lagrangian.1) | data formatting | bytes 1048576

commit v2 on v1

--- a/solution.py
+++ b/solution.py
@@ -22,44 +22,60 @@
 
 def kernel(
     bands, regions, fields, lists, departure, hweight, base_level, vweight, vertical_op, out,
-    own, halo, lists_s, dep_v, hw_v, base_v, vw_v, vop_v, dep_t, hw_t, w_f32, w_hi, w_lo, e_cat, base_t, vw_t, made,
-    in_sem, halo_send, halo_recv, own_sem, send_sem, recv_sem,
+    own, halo, lists_s, dep_v, hw_v, base_v, vw_v, vop_v, dep_t, hw_t, w_hi, w_lo, e_cat, base_t, vw_t, made, near_sum,
+    in_sem, halo_send, halo_recv, own_sem, send_sem, recv_sem, plane_sem,
 ):
     b, r = lax.axis_index("band"), lax.axis_index("region")
     points = fields.shape[0]
     n_fields = fields.shape[1] // LEV
     group = regions // n_fields
     rows = LEV // group
+    plane = min(8, regions // 2)
+    planes = regions // plane
+    z, spot = r // plane, lax.rem(r, plane)
     east, west = lax.rem(r + 1, regions), lax.rem(r + regions - 1, regions)
+
+    def signal(sem, band, region):
+        pl.semaphore_signal(sem, inc=1, device_id=(band, region), device_id_type=MESH)
+
+    barrier = pltpu.get_barrier_semaphore()
+
+    @pl.when(b > 0)
+    def _():
+        signal(barrier, b - 1, r)
+
+    @pl.when(b < bands - 1)
+    def _():
+        signal(barrier, b + 1, r)
+
+    @pl.when(spot == plane - 1)
+    def _():
+        signal(barrier, b, east)
+
+    @pl.when(spot == 0)
+    def _():
+        signal(barrier, b, west)
+
+    def plane_mate(i):
+        return z * plane + lax.rem(spot + i, plane)
+
+    for i in range(1, plane):
+        signal(barrier, b, plane_mate(i))
+    for i in range(1, planes):
+        signal(barrier, b, lax.rem(r + i * plane, regions))
 
     loads = [
         pltpu.make_async_copy(src, dst, in_sem.at[i])
         for i, (src, dst) in enumerate(
-            [(lists, lists_s), (departure, dep_v), (hweight, hw_v), (base_level, base_v), (vweight, vw_v), (vertical_op, vop_v), (fields, own)]
+            [(departure, dep_v), (hweight, hw_v), (lists, lists_s), (base_level, base_v), (vweight, vw_v), (vertical_op, vop_v), (fields, own)]
         )
     ]
     for load in loads:
         load.start()
 
-    barrier = pltpu.get_barrier_semaphore()
-
-    def greet(band, region):
-        pl.semaphore_signal(barrier, inc=1, device_id=(band, region), device_id_type=MESH)
-
-    @pl.when(b > 0)
-    def _():
-        greet(b - 1, r)
-
-    @pl.when(b < bands - 1)
-    def _():
-        greet(b + 1, r)
-
-    def greet_region(i, carry):
-        greet(b, lax.rem(r + i, regions))
-        return carry
-
-    lax.fori_loop(1, regions, greet_region, 0)
-    pl.semaphore_wait(barrier, regions - 1 + jnp.minimum(b, 1) + jnp.minimum(bands - 1 - b, 1))
+    edges = jnp.minimum(b, 1) + jnp.minimum(bands - 1 - b, 1)
+    corners = (1 - jnp.minimum(spot, 1)) + (1 - jnp.minimum(plane - 1 - spot, 1))
+    pl.semaphore_wait(barrier, plane + planes - 2 + edges + corners)
 
     def offset(t):
         return lax.rem(2 + t * (t + 1) // 2, n_fields)
@@ -92,6 +108,8 @@
         return carry
 
     lax.fori_loop(0, n_fields, send_halo, 0)
+    for i in range(1, plane):
+        signal(plane_sem, b, plane_mate(i))
 
     def blank(d):
         def one(t, carry):
@@ -108,13 +126,13 @@
     def _():
         blank(1)
 
-    for load in loads:
+    for load in loads[:3]:
         load.wait()
 
     blocks = points // LANES
     bases = [i * LANES for i in range(blocks)]
     before, after = jnp.maximum(b - 1, 0), jnp.minimum(b + 1, bands - 1)
-    for d, (band, region) in enumerate([(before, r), (after, r), (b, west), (b, east)]):
+    for d, band, region in [(2, b, west), (3, b, east), (0, before, r), (1, after, r)]:
         first, second = (lists_s[band * 4 + d, e, region] for e in range(2))
         part = points + d * points
         for block in range(blocks):
@@ -125,38 +143,51 @@
     stencil = dep_v.shape[0]
 
     def weigh(i, carry):
-        rows_i = pl.ds(pl.multiple_of(i * 8, 8), 8)
+        rows_i = pl.ds(pl.multiple_of(i * 16, 16), 16)
         dep, hw = dep_t[rows_i, :], hw_t[rows_i, :]
-        deps = [jnp.broadcast_to(dep[:, c : c + 1], (8, LANES)) for c in range(stencil)]
-        hws = [jnp.broadcast_to(hw[:, c : c + 1], (8, LANES)) for c in range(stencil)]
         lane = lax.broadcasted_iota(jnp.int32, (8, LANES), 1)
-        for j, base in enumerate(bases):
-            target = lane + base
-            total = jnp.where(deps[0] == target, hws[0], 0.0)
-            for c in range(1, stencil):
-                total = total + jnp.where(deps[c] == target, hws[c], 0.0)
-            w_f32[rows_i, j * LANES : (j + 1) * LANES] = total
+        sides = []
+        for s in range(2):
+            deps = [jnp.broadcast_to(dep[s * 8 : s * 8 + 8, c : c + 1], (8, LANES)) for c in range(stencil)]
+            hws = [jnp.broadcast_to(hw[s * 8 : s * 8 + 8, c : c + 1], (8, LANES)) for c in range(stencil)]
+            totals = []
+            for base in bases:
+                target = lane + base
+                total = jnp.where(deps[0] == target, hws[0], 0.0)
+                for c in range(1, stencil):
+                    total = total + jnp.where(deps[c] == target, hws[c], 0.0)
+                totals.append(total)
+            sides.append(totals)
+        for j in range(len(bases)):
+            hi, lo = halves(jnp.concatenate([sides[0][j], sides[1][j]], axis=0))
+            w_hi[rows_i, j * LANES : (j + 1) * LANES] = hi
+            w_lo[rows_i, j * LANES : (j + 1) * LANES] = lo
         return carry
 
-    lax.fori_loop(0, points // 8, weigh, 0)
-
-    def split(i, carry):
-        rows_i = pl.ds(pl.multiple_of(i * 16, 16), 16)
-        w_hi[rows_i, :], w_lo[rows_i, :] = halves(w_f32[rows_i, :])
-        return carry
-
-    lax.fori_loop(0, points // 16, split, 0)
-
+    lax.fori_loop(0, points // 16, weigh, 0, unroll=4)
+    for load in loads[3:]:
+        load.wait()
     base_t[...] = jnp.transpose(base_v[...])
     for m in range(4):
         vw_t[m] = jnp.transpose(vw_v[m])
     v_hi, v_lo = halves(vop_v[...])
     v_cat = jnp.concatenate([v_hi, v_hi], axis=1)
 
+    def product(first, last):
+        both = jnp.dot(w_hi[:, first:last], e_cat[first:last, :], preferred_element_type=F32)
+        rest = jnp.dot(w_lo[:, first:last], e_cat[first:last, :LEV], preferred_element_type=F32)
+        return both[:, :LEV] + both[:, LEV:] + rest
+
     def one_field(t, carry):
         f = field_of(r, t)
         column = pl.multiple_of(f * LEV, LEV)
+        near = 3 * points
         e_cat[:points, :LEV], e_cat[:points, LEV:] = halves(own[:, pl.ds(column, LEV)])
+        for d in (2, 3):
+            halo_copy(t, d, b, r).wait_recv()
+            part = slice((d - 1) * points, d * points)
+            e_cat[part, :LEV], e_cat[part, LEV:] = halves(halo[t, d])
+        near_sum[...] = product(0, near)
 
         @pl.when(b > 0)
         def _():
@@ -166,14 +197,10 @@
         def _():
             halo_copy(t, 1, b, r).wait_recv()
 
-        halo_copy(t, 2, b, r).wait_recv()
-        halo_copy(t, 3, b, r).wait_recv()
-        for d in range(4):
-            part = slice((d + 1) * points, (d + 2) * points)
+        for d in (0, 1):
+            part = slice((d + 3) * points, (d + 4) * points)
             e_cat[part, :LEV], e_cat[part, LEV:] = halves(halo[t, d])
-        both = jnp.dot(w_hi[...], e_cat[...], preferred_element_type=F32)
-        rest = jnp.dot(w_lo[...], e_cat[:, :LEV], preferred_element_type=F32)
-        horizontal = both[:, :LEV] + both[:, LEV:] + rest
+        horizontal = near_sum[...] + product(near, 5 * points)
         mixed = jnp.zeros((points, LEV), F32)
         for m in range(4):
             picked = jnp.take_along_axis(horizontal, base_t[...] + (m - 1), axis=1, mode="promise_in_bounds")
@@ -183,18 +210,24 @@
         made[t] = lax.dot_general(v_cat, i_cat, NT, preferred_element_type=F32) + lax.dot_general(
             v_lo, i_hi, NT, preferred_element_type=F32
         )
+
+        @pl.when(t == 0)
+        def _():
+            pl.semaphore_wait(plane_sem, plane - 1)
+
         place = pl.ds(pl.multiple_of(r * points, points), points)
 
         def send_rows(i, carry):
             j = lax.rem(i + r, group)
             target = f * group + j
             src = made.at[t, pl.ds(pl.multiple_of(j * rows, rows), rows)]
+            dst = out.at[:, place]
 
             @pl.when(target != r)
             def _():
                 pltpu.make_async_remote_copy(
                     src_ref=src,
-                    dst_ref=out.at[:, place],
+                    dst_ref=dst,
                     send_sem=send_sem,
                     recv_sem=recv_sem,
                     device_id=(b, target),
@@ -203,7 +236,7 @@
 
             @pl.when(target == r)
             def _():
-                pltpu.make_async_copy(src, out.at[:, place], own_sem).start()
+                pltpu.make_async_copy(src, dst, own_sem).start()
 
             return carry
 
@@ -226,7 +259,7 @@
         return carry
 
     lax.fori_loop(0, n_fields, halo_sent, 0)
-    mine = out.at[:, : points]
+    mine = out.at[:, :points]
     pltpu.make_async_copy(mine, mine, own_sem).wait()
     others = out.at[:, : (regions - 1) * points]
     pltpu.make_async_copy(others, others, send_sem).wait()
@@ -243,11 +276,11 @@
         lists = send_list.transpose(0, 2, 3, 1).reshape(bands * 4, 2, regions)
         extended = points * 5
         anywhere = pl.BlockSpec(memory_space=pl.ANY)
-        resident = anywhere
+        rows = width // regions
         return pl.pallas_call(
             functools.partial(kernel, bands, regions),
-            out_shape=jax.ShapeDtypeStruct((width // regions, points * regions), F32),
-            in_specs=[resident] * 7,
+            out_shape=pltpu.VMEM((rows, points * regions), F32),
+            in_specs=[anywhere] * 7,
             out_specs=anywhere,
             scratch_shapes=[
                 pltpu.VMEM((points, width), F32),
@@ -260,25 +293,26 @@
                 pltpu.VMEM(vertical_op.shape, F32),
                 pltpu.VMEM((points, stencil), jnp.int32),
                 pltpu.VMEM((points, stencil), F32),
-                pltpu.VMEM((points, extended), F32),
                 pltpu.VMEM((points, extended), BF16),
                 pltpu.VMEM((points, extended), BF16),
                 pltpu.VMEM((extended, 2 * LEV), BF16),
                 pltpu.VMEM((points, LEV), jnp.int32),
                 pltpu.VMEM((4, points, LEV), F32),
                 pltpu.VMEM((n_fields, LEV, points), F32),
+                pltpu.VMEM((points, LEV), F32),
                 pltpu.SemaphoreType.DMA((7,)),
                 pltpu.SemaphoreType.DMA((n_fields, 4)),
                 pltpu.SemaphoreType.DMA((n_fields, 4)),
                 pltpu.SemaphoreType.DMA,
                 pltpu.SemaphoreType.DMA,
                 pltpu.SemaphoreType.DMA,
+                pltpu.SemaphoreType.REGULAR,
             ],
             compiler_params=pltpu.CompilerParams(
-                collective_id=0, has_side_effects=True, vmem_limit_bytes=63 * 2**20
+                collective_id=0, has_side_effects=True, vmem_limit_bytes=32 * 2**20
             ),
             name="semi_lagrangian",
-        )(fields, lists, departure, hweight, base_level, vweight, vertical_op)
+        )(*[pltpu.with_memory_space_constraint(a, pltpu.HBM) for a in (fields, lists, departure, hweight, base_level, vweight, vertical_op)])
 
     points_last = P(None, ("band", "region"))
     return jax.shard_map(

time: 34.1 us -> 31.4 us (0.921)
  Pallas kernels: 32.1 us -> 30.5 us
  local copies, waits for them, and re-layouts: 1.87 us -> 0.8 us
    pallas_call x1, Pallas kernels: 32.1 us -> 30.5 us  [body(): pl.pallas_call(functools.partial(kernel, bands, regions), out_shape=pltpu...]
    unnamed x1, local copies, waits for them, and re-layouts: 1.87 us -> 0.8 us
where the time goes in v2:
time: 31.4 us; the launch traced here: 31.3 us
  Pallas kernels  30.5 us (97%)
  local copies, waits for them, and re-layouts  0.8 us (3%)
    pallas_call x1, Pallas kernels, body(): pl.pallas_call(functools.partial(kernel, bands, regions), out_shape=pltpu...  30.5 us
    unnamed x1, local copies, waits for them, and re-layouts  0.8 us

profile of v2, /device:TPU:1, one launch (start us, length us, event | category | flops | bytes accessed | tf_op | source)
XLA Modules:
  0.0 31.3 jit_solution(10676830414522784368)
XLA Ops:
  0.0 30.5 %semi_lagrangian.1 = f32[8,16384]{1,0:T(8,128)S(1)} custom-call(f32[256,512]{1,0:T(8,128)} %fields.1, s32[16,2,64]{2,1,0:T(2,128)} %bitcast.3, s32[16,256]{1,0:T(8,128)} %departure.1, f32[16,256]{1,0:T(8,128)} %hweight.1, s32[128,256]{1,0:T(8,128)} %base_level.1, f32[4,128,256]{2,1,0:T(8,128)} %vweight.1, f32[128,128]{1,0:T(8,128)} %vertical_op.1), custom_call_target="tpu_custom_call" | custom-call | tf_op jit(solution)/shard_map/semi_lagrangian/pallas_call | solution.py:280
  30.5 0.8 %copy.9 = f32[8,16384]{1,0:T(8,128)} copy(f32[8,16384]{1,0:T(8,128)S(1)} %semi_lagrangian.1) | data formatting | bytes 1048576

commit v3 on v2

--- a/solution.py
+++ b/solution.py
@@ -23,7 +23,7 @@
 def kernel(
     bands, regions, fields, lists, departure, hweight, base_level, vweight, vertical_op, out,
     own, halo, lists_s, dep_v, hw_v, base_v, vw_v, vop_v, dep_t, hw_t, w_hi, w_lo, e_cat, base_t, vw_t, made, near_sum,
-    in_sem, halo_send, halo_recv, own_sem, send_sem, recv_sem, plane_sem,
+    in_sem, halo_send, halo_recv, own_sem, send_sem, recv_sem, plane_sem, gate_sem,
 ):
     b, r = lax.axis_index("band"), lax.axis_index("region")
     points = fields.shape[0]
@@ -33,6 +33,7 @@
     plane = min(8, regions // 2)
     planes = regions // plane
     z, spot = r // plane, lax.rem(r, plane)
+    gate = plane // 2
     east, west = lax.rem(r + 1, regions), lax.rem(r + regions - 1, regions)
 
     def signal(sem, band, region):
@@ -61,8 +62,11 @@
 
     for i in range(1, plane):
         signal(barrier, b, plane_mate(i))
-    for i in range(1, planes):
-        signal(barrier, b, lax.rem(r + i * plane, regions))
+
+    @pl.when(spot == gate)
+    def _():
+        for i in range(1, planes):
+            signal(barrier, b, lax.rem(r + i * plane, regions))
 
     loads = [
         pltpu.make_async_copy(src, dst, in_sem.at[i])
@@ -75,13 +79,12 @@
 
     edges = jnp.minimum(b, 1) + jnp.minimum(bands - 1 - b, 1)
     corners = (1 - jnp.minimum(spot, 1)) + (1 - jnp.minimum(plane - 1 - spot, 1))
-    pl.semaphore_wait(barrier, plane + planes - 2 + edges + corners)
-
-    def offset(t):
-        return lax.rem(2 + t * (t + 1) // 2, n_fields)
+    at_gate = jnp.where(spot == gate, 1, 0)
+    pl.semaphore_wait(barrier, plane - 1 + at_gate * (planes - 1) + edges + corners)
 
     def field_of(region, t):
-        return lax.rem(region // group + offset(t), n_fields)
+        pair = region // group
+        return 2 * lax.rem(pair // 2 + 1 + t // 2, 2) + lax.rem(pair + t + t // 2, 2)
 
     def halo_copy(t, d, band, region):
         column = pl.multiple_of(field_of(region, t) * LEV, LEV)
@@ -108,8 +111,14 @@
         return carry
 
     lax.fori_loop(0, n_fields, send_halo, 0)
-    for i in range(1, plane):
-        signal(plane_sem, b, plane_mate(i))
+
+    @pl.when(spot == gate)
+    def _():
+        for i in range(1, planes):
+            signal(gate_sem, b, lax.rem(r + i * plane, regions))
+        pl.semaphore_wait(gate_sem, planes - 1)
+        for i in range(1, plane):
+            signal(plane_sem, b, plane_mate(i))
 
     def blank(d):
         def one(t, carry):
@@ -211,16 +220,15 @@
             v_lo, i_hi, NT, preferred_element_type=F32
         )
 
-        @pl.when(t == 0)
-        def _():
-            pl.semaphore_wait(plane_sem, plane - 1)
+        @pl.when((t == 0) & (spot != gate))
+        def _():
+            pl.semaphore_wait(plane_sem, 1)
 
         place = pl.ds(pl.multiple_of(r * points, points), points)
 
         def send_rows(i, carry):
-            j = lax.rem(i + r, group)
-            target = f * group + j
-            src = made.at[t, pl.ds(pl.multiple_of(j * rows, rows), rows)]
+            target = f * group + i
+            src = made.at[t, pl.ds(pl.multiple_of(i * rows, rows), rows)]
             dst = out.at[:, place]
 
             @pl.when(target != r)
@@ -307,6 +315,7 @@
                 pltpu.SemaphoreType.DMA,
                 pltpu.SemaphoreType.DMA,
                 pltpu.SemaphoreType.REGULAR,
+                pltpu.SemaphoreType.REGULAR,
             ],
             compiler_params=pltpu.CompilerParams(
                 collective_id=0, has_side_effects=True, vmem_limit_bytes=32 * 2**20

time: 31.4 us -> 28.9 us (0.920)
  Pallas kernels: 30.5 us -> 28 us
    pallas_call x1, Pallas kernels: 30.5 us -> 28 us  [body(): pl.pallas_call(functools.partial(kernel, bands, regions), out_shape=pltpu...]
where the time goes in v3:
time: 28.9 us; the launch traced here: 28.8 us
  Pallas kernels  28 us (97%)
  local copies, waits for them, and re-layouts  0.8 us (3%)
    pallas_call x1, Pallas kernels, body(): pl.pallas_call(functools.partial(kernel, bands, regions), out_shape=pltpu...  28 us
    unnamed x1, local copies, waits for them, and re-layouts  0.8 us

profile of v3, /device:TPU:1, one launch (start us, length us, event | category | flops | bytes accessed | tf_op | source)
XLA Modules:
  0.0 28.8 jit_solution(10430884152049917635)
XLA Ops:
  0.0 28.0 %semi_lagrangian.1 = f32[8,16384]{1,0:T(8,128)S(1)} custom-call(f32[256,512]{1,0:T(8,128)} %fields.1, s32[16,2,64]{2,1,0:T(2,128)} %bitcast.3, s32[16,256]{1,0:T(8,128)} %departure.1, f32[16,256]{1,0:T(8,128)} %hweight.1, s32[128,256]{1,0:T(8,128)} %base_level.1, f32[4,128,256]{2,1,0:T(8,128)} %vweight.1, f32[128,128]{1,0:T(8,128)} %vertical_op.1), custom_call_target="tpu_custom_call" | custom-call | tf_op jit(solution)/shard_map/semi_lagrangian/pallas_call | solution.py:288
  28.0 0.8 %copy.9 = f32[8,16384]{1,0:T(8,128)} copy(f32[8,16384]{1,0:T(8,128)S(1)} %semi_lagrangian.1) | data formatting | bytes 1048576

commit v4 on v3

--- a/solution.py
+++ b/solution.py
@@ -77,6 +77,21 @@
     for load in loads:
         load.start()
 
+    def blank(d):
+        def one(t, carry):
+            halo[t, d] = jnp.zeros(halo.shape[2:], F32)
+            return carry
+
+        lax.fori_loop(0, n_fields, one, 0)
+
+    @pl.when(b == 0)
+    def _():
+        blank(0)
+
+    @pl.when(b == bands - 1)
+    def _():
+        blank(1)
+
     edges = jnp.minimum(b, 1) + jnp.minimum(bands - 1 - b, 1)
     corners = (1 - jnp.minimum(spot, 1)) + (1 - jnp.minimum(plane - 1 - spot, 1))
     at_gate = jnp.where(spot == gate, 1, 0)
@@ -84,7 +99,8 @@
 
     def field_of(region, t):
         pair = region // group
-        return 2 * lax.rem(pair // 2 + 1 + t // 2, 2) + lax.rem(pair + t + t // 2, 2)
+        flip = (pair // 3) * (1 - t // 2)
+        return 2 * lax.rem(pair // 2 + 1 + t // 2, 2) + lax.rem(pair + t + t // 2 + flip, 2)
 
     def halo_copy(t, d, band, region):
         column = pl.multiple_of(field_of(region, t) * LEV, LEV)
@@ -110,30 +126,13 @@
         halo_copy(t, 3, b, west).start()
         return carry
 
-    lax.fori_loop(0, n_fields, send_halo, 0)
-
     @pl.when(spot == gate)
     def _():
         for i in range(1, planes):
             signal(gate_sem, b, lax.rem(r + i * plane, regions))
-        pl.semaphore_wait(gate_sem, planes - 1)
-        for i in range(1, plane):
-            signal(plane_sem, b, plane_mate(i))
-
-    def blank(d):
-        def one(t, carry):
-            halo[t, d] = jnp.zeros(halo.shape[2:], F32)
-            return carry
-
-        lax.fori_loop(0, n_fields, one, 0)
-
-    @pl.when(b == 0)
-    def _():
-        blank(0)
-
-    @pl.when(b == bands - 1)
-    def _():
-        blank(1)
+
+    lax.fori_loop(0, n_fields, send_halo, 0)
+
 
     for load in loads[:3]:
         load.wait()
@@ -174,6 +173,13 @@
         return carry
 
     lax.fori_loop(0, points // 16, weigh, 0, unroll=4)
+
+    @pl.when(spot == gate)
+    def _():
+        pl.semaphore_wait(gate_sem, planes - 1)
+        for i in range(1, plane):
+            signal(plane_sem, b, plane_mate(i))
+
     for load in loads[3:]:
         load.wait()
     base_t[...] = jnp.transpose(base_v[...])
@@ -226,7 +232,8 @@
 
         place = pl.ds(pl.multiple_of(r * points, points), points)
 
-        def send_rows(i, carry):
+        def send_rows(step, carry):
+            i = step // 2 + lax.rem(step, 2) * (group // 2)
             target = f * group + i
             src = made.at[t, pl.ds(pl.multiple_of(i * rows, rows), rows)]
             dst = out.at[:, place]

time: 28.9 us -> 28.5 us (0.986)
  the two profiles are of different devices: /device:TPU:1 before, /device:TPU:69 now
where the time goes in v4:
time: 28.5 us; the launch traced here: 28.4 us
  Pallas kernels  27.6 us (97%)
  local copies, waits for them, and re-layouts  0.8 us (3%)
    pallas_call x1, Pallas kernels, body(): pl.pallas_call(functools.partial(kernel, bands, regions), out_shape=pltpu...  27.6 us
    unnamed x1, local copies, waits for them, and re-layouts  0.8 us

profile of v4, /device:TPU:69, one launch (start us, length us, event | category | flops | bytes accessed | tf_op | source)
XLA Modules:
  0.0 28.4 jit_solution(14021661378213993118)
XLA Ops:
  0.0 27.6 %semi_lagrangian.1 = f32[8,16384]{1,0:T(8,128)S(1)} custom-call(f32[256,512]{1,0:T(8,128)} %fields.1, s32[16,2,64]{2,1,0:T(2,128)} %bitcast.3, s32[16,256]{1,0:T(8,128)} %departure.1, f32[16,256]{1,0:T(8,128)} %hweight.1, s32[128,256]{1,0:T(8,128)} %base_level.1, f32[4,128,256]{2,1,0:T(8,128)} %vweight.1, f32[128,128]{1,0:T(8,128)} %vertical_op.1), custom_call_target="tpu_custom_call" | custom-call | tf_op jit(solution)/shard_map/semi_lagrangian/pallas_call | solution.py:295
  27.6 0.8 %copy.9 = f32[8,16384]{1,0:T(8,128)} copy(f32[8,16384]{1,0:T(8,128)S(1)} %semi_lagrangian.1) | data formatting | bytes 1048576

commit v5 on v4

--- a/solution.py
+++ b/solution.py
@@ -186,7 +186,7 @@
     for m in range(4):
         vw_t[m] = jnp.transpose(vw_v[m])
     v_hi, v_lo = halves(vop_v[...])
-    v_cat = jnp.concatenate([v_hi, v_hi], axis=1)
+    v_cat = jnp.concatenate([jnp.concatenate([v, v], axis=1) for v in (v_hi, v_lo)], axis=0)
 
     def product(first, last):
         both = jnp.dot(w_hi[:, first:last], e_cat[first:last, :], preferred_element_type=F32)
@@ -222,9 +222,8 @@
             mixed = mixed + vw_t[m] * picked
         i_hi, i_lo = halves(mixed)
         i_cat = jnp.concatenate([i_hi, i_lo], axis=1)
-        made[t] = lax.dot_general(v_cat, i_cat, NT, preferred_element_type=F32) + lax.dot_general(
-            v_lo, i_hi, NT, preferred_element_type=F32
-        )
+        operated = lax.dot_general(v_cat, i_cat, NT, preferred_element_type=F32)
+        made[t] = operated[:LEV] + operated[LEV:]
 
         @pl.when((t == 0) & (spot != gate))
         def _():

time: 28.5 us -> 28.5 us (level)
  no operation moved by 1% of the time
where the time goes in v5:
time: 28.5 us
  Pallas kernels  27.7 us (97%)
  local copies, waits for them, and re-layouts  0.8 us (3%)
    pallas_call x1, Pallas kernels, body(): pl.pallas_call(functools.partial(kernel, bands, regions), out_shape=pltpu...  27.7 us
    unnamed x1, local copies, waits for them, and re-layouts  0.8 us

profile of v5, /device:TPU:69, one launch (start us, length us, event | category | flops | bytes accessed | tf_op | source)
XLA Modules:
  0.0 28.5 jit_solution(1433926587833580812)
XLA Ops:
  0.0 27.7 %semi_lagrangian.1 = f32[8,16384]{1,0:T(8,128)S(1)} custom-call(f32[256,512]{1,0:T(8,128)} %fields.1, s32[16,2,64]{2,1,0:T(2,128)} %bitcast.3, s32[16,256]{1,0:T(8,128)} %departure.1, f32[16,256]{1,0:T(8,128)} %hweight.1, s32[128,256]{1,0:T(8,128)} %base_level.1, f32[4,128,256]{2,1,0:T(8,128)} %vweight.1, f32[128,128]{1,0:T(8,128)} %vertical_op.1), custom_call_target="tpu_custom_call" | custom-call | tf_op jit(solution)/shard_map/semi_lagrangian/pallas_call | solution.py:294
  27.7 0.8 %copy.9 = f32[8,16384]{1,0:T(8,128)} copy(f32[8,16384]{1,0:T(8,128)S(1)} %semi_lagrangian.1) | data formatting | bytes 1048576
